TPU v7x, 128 devices: a whole 4x4x4 slice. The times are simulated.
128 devices in a mesh: rcv: 8 (over z, core), src: 16 (over y, x).
Axes of the slice: x: 4, y: 4, z: 4, core: 2. Of those that a mesh axis runs over, the one named last changes fastest.
Arguments:
- response: float32 [8, 8192, 8192], P(None, 'rcv', 'src'), may hold values from -0.0234375 to 0.0234375
- focusing: float32 [16, 71, 8192], P(None, None, ('src', 'rcv')), may hold values from -6 to 6
Outputs:
- convolved: float32 [64, 16, 8192], P('src', None, 'rcv')
All inputs are finite; a program needn't handle non-finite values.
Results may differ from a plain program's by a relative error of at most 0.00011.
Values sent between devices are 32-bit elements; how exact they have to be, the bound alone decides.
A program may use at most 64 MiB of HBM per device.

v0:
```python
import jax
import jax.numpy as jnp
from jax import lax
from jax.sharding import PartitionSpec as P


def lagged_block(history, taps):
    shifted = jnp.transpose(history, (1, 0, 2))
    steps_out = shifted.shape[0] - taps + 1
    return jnp.stack(
        [shifted[taps - 1 - k : taps - 1 - k + steps_out] for k in range(taps)], axis=2
    )


def apply_band(lags, band):
    return lax.dot_general(
        lags,
        band,
        (((2, 3), (0, 2)), ((), ())),
        precision=lax.Precision.HIGHEST,
        preferred_element_type=jnp.float32,
    )


def on_device(response, focusing):
    taps = response.shape[0]
    history = lax.all_gather(focusing, "rcv", axis=2, tiled=True)
    partial_out = apply_band(lagged_block(history, taps), response)
    return lax.psum_scatter(partial_out, "src", scatter_dimension=0, tiled=True)


def solution(mesh):
    in_specs = (P(None, "rcv", "src"), P(None, None, ("src", "rcv")))
    out_specs = P("src", None, "rcv")
    return jax.shard_map(
        on_device, mesh=mesh, in_specs=in_specs, out_specs=out_specs, check_vma=False
    )
```

profile of v0, /device:TPU:0, one launch (start us, length us, event | category | flops | bytes accessed | tf_op | source)
XLA Modules:
  0.0 192.0 jit_solution(12918974599513108388)
XLA Ops:
  6.5 0.0 all-gather.2.cloned.1.call-start
  6.5 2.2 %copy.11 = f32[16,71,64]{1,0,2:T(8,128)} copy(f32[16,71,64]{1,2,0:T(8,128)} %param.3) | data formatting | bytes 581632 | tf_op args[1]
  8.7 0.0 all-gather.2.cloned.1.call-update
  8.7 0.0 reduce-scatter.2.cloned.1.call-start
  8.8 35.1 %all-gather.2.cloned.1.call-done = f32[16,71,512]{1,0,2:T(8,128)} async-done(((f32[16,71,64]{1,0,2:T(8,128)}), f32[16,71,512]{1,0,2:T(8,128)}) %all-gather.2.cloned.1.call-update) | async-done | bytes 2326544 | tf_op jit(solution)/shard_map/all_gather | solution.py:27
  43.9 3.8 %copy.12 = f32[16,71,512]{2,0,1:T(8,128)S(1)} copy(f32[16,71,512]{1,0,2:T(8,128)} %all-gather.2.cloned.1.call-done) | data formatting | bytes 4653056 | tf_op jit(solution)/shard_map/all_gather | solution.py:27
  47.7 0.2 fusion.12
  47.9 0.2 fusion.11
  48.1 0.2 fusion.10
  48.3 0.2 fusion.9
  48.5 0.2 fusion.8
  48.7 0.2 fusion.7
  48.9 0.2 fusion.6
  49.1 0.2 fusion.5
  49.3 58.4 %fusion.2 = f32[64,16,1024]{2,1,0:T(8,128)} fusion(f32[64,16,8,512]{3,1,2,0:T(8,128)S(1)} %fusion.5, f32[8,1024,512]{2,1,0:T(8,128)} %param.2), kind=kOutput, calls=%fused_computation.2 | convolution fusion | flops 51539607552 | bytes 37748736 | tf_op jit(solution)/shard_map/dot_general | solution.py:16
  107.7 0.0 reduce-scatter.2.cloned.1.call-update
  107.7 77.4 %reduce-scatter.2.cloned.1.call-done = f32[4,16,1024]{2,1,0:T(8,128)} async-done(((f32[64,16,1024]{2,1,0:T(8,128)}), f32[4,16,1024]{2,1,0:T(8,128)}) %reduce-scatter.2.cloned.1.call-update) | async-done | bytes 262160 | tf_op jit(solution)/shard_map/reduce_scatter | solution.py:29
Async XLA Ops:
  6.5 37.4 %all-gather.2.cloned.1.call-start = ((), (), s32[]{:S(2)}) async-start(), calls=%async_computation.1 | async-start | bytes 4718592 | tf_op jit(solution)/shard_map/all_gather | solution.py:27
  8.7 176.4 %reduce-scatter.2.cloned.1.call-start = ((), (), s32[]{:S(2)}) async-start(), calls=%async_computation.2 | async-start | bytes 4456448 | tf_op jit(solution)/shard_map/reduce_scatter | solution.py:29
Sparse Core Ops, SparseCore 0:
  9.1 34.7 all-gather.1
  107.8 77.2 reduce-scatter.1
where the time goes:
time: 192 us
  waiting for transfers between devices  113 us (59%)
  matrix products  58.4 us (30%)
  between operations  13.5 us (7%)
  local copies, waits for them, and re-layouts  7.46 us (4%)
    reduce_scatter x1, waiting for transfers between devices, on_device(): return lax.psum_scatter(partial_out, 'src', scatter_dimension=0, tiled=True)  77.4 us
    dot_general x1, matrix products, apply_band(): lax.dot_general(lags, band, (((2, 3), (0, 2)), ((), ())), precision=lax.P...  58.4 us
    all_gather x1, waiting for transfers between devices, on_device(): history = lax.all_gather(focusing, 'rcv', axis=2, tiled=True)  35.1 us
  transfers between devices with their start and end apart: 2, of which 2 were waited for; matrix products, arithmetic and copies ran while one was open for 0% of the time, Pallas kernels for 0%

commit v1 on v0

v1 whole, which is shorter than its diff:
```python
import jax
import jax.numpy as jnp
from jax import lax
from jax.experimental import pallas as pl
from jax.experimental.pallas import tpu as pltpu
from jax.sharding import PartitionSpec as P

MESH = pl.DeviceIdType.MESH
F32, BF16 = jnp.float32, jnp.bfloat16
OFFSETS = (0, 1, 3, 2)
NT = (((1,), (1,)), ((), ()))


def split(v):
    high = v.astype(BF16)
    return high, (v - high.astype(F32)).astype(BF16)


def kernel(resp, foc, out, raw, band, hist, flat, lags, part, got1, got2,
           raw_sem, z_send, pair_send, hist_recv, send1, recv1, send2, recv2):
    rcv, src = lax.axis_index("rcv"), lax.axis_index("src")
    z, core = rcv // 2, lax.rem(rcv, 2)
    y, x = src // 4, lax.rem(src, 4)

    def along_z(d):
        return {"rcv": lax.rem(z + d, 4) * 2 + core}

    def along_x(d):
        return {"src": y * 4 + lax.rem(x + d, 4)}

    def along_y(d):
        return {"src": lax.rem(y + d, 4) * 4 + x}

    pair = {"rcv": z * 2 + 1 - core}
    partners = [pair] + [f(d) for f in (along_z, along_x, along_y) for d in (1, 2, 3)]

    barrier = pltpu.get_barrier_semaphore()
    for device in partners:
        pl.semaphore_signal(barrier, inc=1, device_id=device, device_id_type=MESH)

    def fetch(place, slot):
        lanes = pl.multiple_of(lax.rem(z + OFFSETS[place], 4) * 128, 128)
        return pltpu.make_async_copy(resp.at[:, :, pl.ds(lanes, 128)], raw.at[slot], raw_sem.at[place])

    for place in range(2):
        fetch(place, place).start()

    def remote(src_ref, dst_ref, send, recv, device):
        return pltpu.make_async_remote_copy(
            src_ref=src_ref, dst_ref=dst_ref, send_sem=send, recv_sem=recv,
            device_id=device, device_id_type=MESH)

    for f in range(16):
        steps = foc[f].T
        both = jnp.concatenate([steps[0:36, :], steps[35:71, :]], axis=1)
        hist[f // 8, 0, 0, pl.ds(f % 8, 36, stride=8), :] = both

    def to_z(h, d):
        return remote(hist.at[h, 0, 0], hist.at[h, (4 - d) % 4, 0], z_send.at[h, d - 1],
                      hist_recv.at[h, (4 - d) % 4, 0], along_z(d))

    def to_pair(h, o):
        return remote(hist.at[h, o, 0], hist.at[h, o, 1], pair_send.at[h, o], hist_recv.at[h, o, 1], pair)

    pl.semaphore_wait(barrier, len(partners))
    for h in range(2):
        to_pair(h, 0).start()
        for d in (1, 3, 2):
            to_z(h, d).start()

    def split_band(place, slot, block, rows):
        for r in range(0, rows, 32):
            at = pl.ds(pl.multiple_of(block * rows + r, 32), 32)
            for j in range(4):
                first, second = raw[slot, j, at, :], raw[slot, 4 + j, at, :]
                lanes = pl.ds(place * 512 + j * 128, 128)
                for p, v in enumerate((first + second, second, first)):
                    high, low = split(v)
                    band[p, 0, at, lanes] = high
                    band[p, 1, at, lanes] = low

    def split_lags(h, place):
        o = OFFSETS[place]
        lane = lax.broadcasted_iota(jnp.int32, (288, 128), 1)
        a, b = hist[h, o, core], hist[h, o, 1 - core]
        flat[0:288, :] = jnp.where(lane < 64, a, pltpu.roll(b, 64, 1))
        flat[280:568, :] = jnp.where(lane < 64, pltpu.roll(a, 64, 1), b)
        for j in range(4):
            lanes = pl.ds(place * 512 + j * 128, 128)

            def window(m, _):
                at = pl.ds(pl.multiple_of(m * 32, 32), 32)

                def rows(t):
                    return flat[pl.ds(pl.multiple_of(m * 64 + t * 8, 8), 32), :]

                now = rows(7 - j)
                for p, v in enumerate((now, rows(3 - j) - now, now - rows(11 - j))):
                    high, low = split(v)
                    lags[h, p, 0, at, lanes] = high
                    lags[h, p, 1, at, lanes] = low
                return 0

            lax.fori_loop(0, 8, window, 0)

    def product(h, quarter, p, first, last):
        at = pl.ds(pl.multiple_of(quarter * 256, 256), 256)
        lanes = pl.ds(first * 512, (last - first) * 512)
        total = None
        for i, j in ((0, 0), (0, 1), (1, 0)):
            term = lax.dot_general(lags[h, p, i, :, lanes], band[p, j, at, lanes], NT, preferred_element_type=F32)
            total = term if total is None else total + term
        return total

    def add_products(h, quarter, first, last, fresh):
        chunk = h * 4 + quarter
        for p, odds in ((0, (0, 1)), (1, (0,)), (2, (1,))):
            total = product(h, quarter, p, first, last)
            for m in range(8):
                for b in odds:
                    to_x, to_y = 2 * (m % 2) + b, m // 2
                    block = total[m * 32:(m + 1) * 32, :]
                    for way, (one, two) in enumerate(((to_x, to_y), (to_y, to_x))):
                        v = block[:, way * 128:(way + 1) * 128]
                        if p == 2:
                            v = part[chunk, way, one, two] - v
                        elif p == 1 or not fresh:
                            v = part[chunk, way, one, two] + v
                        part[chunk, way, one, two] = v

    lanes_of = (x, y)
    ring1, ring2 = (along_x, along_y), (along_y, along_x)

    def stage1(chunk, way, d):
        return remote(part.at[chunk, way, lax.rem(lanes_of[way] + d, 4)], got1.at[chunk, way, d - 1],
                      send1.at[chunk, way, d - 1], recv1.at[chunk, way, d - 1], ring1[way](d))

    def stage2(chunk, way, d):
        return remote(part.at[chunk, way, lanes_of[way], lax.rem(lanes_of[1 - way] + d, 4)], got2.at[chunk, way, d - 1],
                      send2.at[chunk, way, d - 1], recv2.at[chunk, way, d - 1], ring2[way](d))

    def begin(chunk):
        for d in (2, 1, 3):
            for way in range(2):
                stage1(chunk, way, d).start()

    def turn(chunk):
        for way in range(2):
            for d in (1, 3, 2):
                stage1(chunk, way, d).wait_recv()
            part[chunk, way, lanes_of[way]] += got1[chunk, way, 0] + (got1[chunk, way, 1] + got1[chunk, way, 2])
            for d in (2, 1, 3):
                stage2(chunk, way, d).start()

    def finish(h, quarter):
        chunk = h * 4 + quarter
        for way in range(2):
            for d in (1, 3, 2):
                stage2(chunk, way, d).wait_recv()
            v = ((part[chunk, way, lanes_of[way], lanes_of[1 - way]] + got2[chunk, way, 0])
                 + (got2[chunk, way, 1] + got2[chunk, way, 2]))
            out[:, h * 8:(h + 1) * 8, quarter * 256 + way * 128:quarter * 256 + way * 128 + 128] = v.reshape(4, 8, 128)

    fetch(0, 0).wait()
    lax.fori_loop(0, 8, lambda i, _: (split_band(0, 0, i, 128), 0)[1], 0)
    fetch(2, 0).start()
    to_pair(0, 0).wait_recv()
    split_lags(0, 0)
    fetch(1, 1).wait()

    def own(h, first, place, rows):
        def step(i, _):
            add_products(h, first + i, 0, 1, True)
            split_band(place, (place % 2), i, rows)
            return 0
        return step

    lax.fori_loop(0, 4, own(0, 0, 1, 256), 0)
    fetch(3, 1).start()
    to_pair(1, 0).wait_recv()
    split_lags(1, 0)
    fetch(2, 0).wait()
    lax.fori_loop(0, 2, own(1, 0, 2, 512), 0)
    fetch(3, 1).wait()
    lax.fori_loop(0, 2, own(1, 2, 3, 512), 0)

    def pass_on(h):
        for d in (1, 3, 2):
            to_z(h, d).wait_recv()
        for place in (1, 2, 3):
            to_pair(h, OFFSETS[place]).start()
        for place in (1, 2, 3):
            to_pair(h, OFFSETS[place]).wait_recv()
            split_lags(h, place)

    def rest(h):
        def step(i, _):
            chunk = h * 4 + i
            add_products(h, i, 1, 4, False)
            begin(chunk)

            @pl.when(chunk >= 2)
            def _():
                turn(chunk - 2)
            return 0

        lax.fori_loop(0, 4, step, 0)

    pass_on(0)
    rest(0)
    pass_on(1)
    rest(1)
    turn(6)
    turn(7)
    for h in range(2):
        for quarter in range(4):
            finish(h, quarter)

    for h in range(2):
        for d in (1, 2, 3):
            to_z(h, d).wait_send()
        for o in range(4):
            to_pair(h, o).wait_send()

    def drain(chunk, _):
        for way in range(2):
            for d in (1, 2, 3):
                stage1(chunk, way, d).wait_send()
                stage2(chunk, way, d).wait_send()
        return 0

    lax.fori_loop(0, 8, drain, 0)


def on_device(response, focusing):
    dma = pltpu.SemaphoreType.DMA
    return pl.pallas_call(
        kernel,
        out_shape=jax.ShapeDtypeStruct((4, 16, 1024), F32),
        in_specs=[pl.BlockSpec(memory_space=pl.ANY), pl.BlockSpec(memory_space=pltpu.VMEM)],
        out_specs=pl.BlockSpec(memory_space=pltpu.VMEM),
        scratch_shapes=[
            pltpu.VMEM((2, 8, 1024, 128), F32),
            pltpu.VMEM((3, 2, 1024, 2048), BF16),
            pltpu.VMEM((2, 4, 2, 288, 128), F32),
            pltpu.VMEM((568, 128), F32),
            pltpu.VMEM((2, 3, 2, 256, 2048), BF16),
            pltpu.VMEM((8, 2, 4, 4, 32, 128), F32),
            pltpu.VMEM((8, 2, 3, 4, 32, 128), F32),
            pltpu.VMEM((8, 2, 3, 32, 128), F32),
            dma((4,)), dma((2, 3)), dma((2, 4)), dma((2, 4, 2)),
            dma((8, 2, 3)), dma((8, 2, 3)), dma((8, 2, 3)), dma((8, 2, 3)),
        ],
        compiler_params=pltpu.CompilerParams(
            collective_id=0, has_side_effects=True, vmem_limit_bytes=63 * 2**20),
    )(response, jnp.swapaxes(focusing, 1, 2))


def solution(mesh):
    in_specs = (P(None, "rcv", "src"), P(None, None, ("src", "rcv")))
    return jax.shard_map(
        on_device, mesh=mesh, in_specs=in_specs, out_specs=P("src", None, "rcv"), check_vma=False
    )
```

time: 192 us -> 65.7 us (0.34)
  waiting for transfers between devices: 113 us -> 0 us
  Pallas kernels: 0 us -> 63.8 us
  matrix products: 58.4 us -> 0 us
  between operations: 13.5 us -> 0.01 us
  local copies, waits for them, and re-layouts: 7.46 us -> 1.67 us
    reduce_scatter x1 -> x0, waiting for transfers between devices: 77.4 us -> none  [on_device(): return lax.psum_scatter(partial_out, 'src', scatter_dimension=0, tiled=True)]
    pallas_call x0 -> x1, Pallas kernels: none -> 63.8 us  [on_device(): pl.pallas_call(kernel, out_shape=jax.ShapeDtypeStruct((4, 16, 1024), F32)...]
    dot_general x1 -> x0, matrix products: 58.4 us -> none  [apply_band(): lax.dot_general(lags, band, (((2, 3), (0, 2)), ((), ())), precision=lax.P...]
    all_gather x1 -> x0, waiting for transfers between devices: 35.1 us -> none  [on_device(): history = lax.all_gather(focusing, 'rcv', axis=2, tiled=True)]
    all_gather x1 -> x0, local copies, waits for them, and re-layouts: 3.83 us -> none  [on_device(): history = lax.all_gather(focusing, 'rcv', axis=2, tiled=True)]
  transfers between devices with their start and end apart: 2 -> 0, of which waited for: 2 -> 0; matrix products, arithmetic and copies ran while one was open for 0% -> 0% of each run, Pallas kernels for 0% -> 0%
where the time goes in v1:
time: 65.7 us; the launch traced here: 65.5 us
  Pallas kernels  63.8 us (97%)
  local copies, waits for them, and re-layouts  1.67 us (3%)
    pallas_call x1, Pallas kernels, on_device(): pl.pallas_call(kernel, out_shape=jax.ShapeDtypeStruct((4, 16, 1024), F32)...  63.8 us
    unnamed x1, local copies, waits for them, and re-layouts  1.67 us

profile of v1, /device:TPU:0, one launch (start us, length us, event | category | flops | bytes accessed | tf_op | source)
XLA Modules:
  0.0 65.5 jit_solution(9446096248893902205)
XLA Ops:
  0.0 63.8 %shard_map.28 = f32[4,16,1024]{2,1,0:T(8,128)} custom-call(f32[8,1024,512]{2,1,0:T(8,128)} %resp.1, f32[16,64,71]{2,1,0:T(8,128)} %bitcast.1), custom_call_target="tpu_custom_call" | custom-call | tf_op jit(solution)/shard_map/pallas_call | solution.py:237
  63.8 1.7 %copy.4 = f32[4,16,1024]{2,1,0:T(8,128)} copy(f32[4,16,1024]{2,1,0:T(8,128)} %shard_map.28) | data formatting | bytes 524288

commit v2 on v1

v2 whole, which is shorter than its diff:
```python
import jax
import jax.numpy as jnp
from jax import lax
from jax.experimental import pallas as pl
from jax.experimental.pallas import tpu as pltpu
from jax.sharding import PartitionSpec as P

MESH = pl.DeviceIdType.MESH
F32, BF16 = jnp.float32, jnp.bfloat16
OFFSETS = (0, 1, 3, 2)
NT = (((1,), (1,)), ((), ()))


def split(v):
    high = v.astype(BF16)
    return high, (v - high.astype(F32)).astype(BF16)


def kernel(resp, foc, out, raw, band, hist, flat, lags, part, got1, got2,
           raw_sem, z_send, pair_send, hist_recv, send1, recv1, send2, recv2):
    rcv, src = lax.axis_index("rcv"), lax.axis_index("src")
    z, core = rcv // 2, lax.rem(rcv, 2)
    y, x = src // 4, lax.rem(src, 4)

    xs, ys, zs = ([lax.rem(v + d, 4) for d in range(4)] for v in (x, y, z))
    on_x = [{"src": y * 4 + v, "rcv": rcv} for v in xs]
    on_y = [{"src": v * 4 + x, "rcv": rcv} for v in ys]
    on_z = [{"src": src, "rcv": v * 2 + core} for v in zs]
    pair = {"src": src, "rcv": z * 2 + 1 - core}
    partners = [pair] + on_z[1:] + on_x[1:] + on_y[1:]

    barrier = pltpu.get_barrier_semaphore()
    for device in partners:
        pl.semaphore_signal(barrier, inc=1, device_id=device, device_id_type=MESH)

    def fetch(place, slot):
        lanes = pl.multiple_of(zs[OFFSETS[place]] * 128, 128)
        return pltpu.make_async_copy(resp.at[:, :, pl.ds(lanes, 128)], raw.at[slot], raw_sem.at[place])

    for place in range(2):
        fetch(place, place).start()

    def remote(src_ref, dst_ref, send, recv, device):
        return pltpu.make_async_remote_copy(
            src_ref=src_ref, dst_ref=dst_ref, send_sem=send, recv_sem=recv,
            device_id=device, device_id_type=MESH)

    for f in range(16):
        steps = foc[f].T
        both = jnp.concatenate([steps[0:36, :], steps[35:71, :]], axis=1)
        hist[f // 8, 0, 0, pl.ds(f % 8, 36, stride=8), :] = both

    def to_z(h, d):
        return remote(hist.at[h, 0, 0], hist.at[h, (4 - d) % 4, 0], z_send.at[h, d - 1],
                      hist_recv.at[h, (4 - d) % 4, 0], on_z[d])

    def to_pair(h, o):
        return remote(hist.at[h, o, 0], hist.at[h, o, 1], pair_send.at[h, o], hist_recv.at[h, o, 1], pair)

    def split_band(place, slot):
        def step(i, _):
            for r in range(8):
                at = pl.ds(pl.multiple_of(i * 128 + r * 16, 16), 16)
                for j in range(4):
                    first, second = raw[slot, j, at, :], raw[slot, 4 + j, at, :]
                    lanes = pl.ds(place * 512 + j * 128, 128)
                    for p, v in enumerate((first + second, second, first)):
                        high, low = split(v)
                        band[p, 0, at, lanes] = high
                        band[p, 1, at, lanes] = low
            return 0

        lax.fori_loop(0, 8, step, 0)

    def split_lags(h, place):
        o = OFFSETS[place]
        lane = lax.broadcasted_iota(jnp.int32, (288, 128), 1)
        a, b = hist[h, o, core], hist[h, o, 1 - core]
        flat[0:288, :] = jnp.where(lane < 64, a, pltpu.roll(b, 64, 1))
        flat[280:568, :] = jnp.where(lane < 64, pltpu.roll(a, 64, 1), b)

        def window(m, _):
            at = pl.ds(pl.multiple_of(m * 32, 32), 32)

            def rows(t):
                return flat[pl.ds(pl.multiple_of(m * 64 + t * 8, 8), 32), :]

            for j in range(4):
                lanes = pl.ds(place * 512 + j * 128, 128)
                now = rows(7 - j)
                for p, v in enumerate((now, rows(3 - j) - now, now - rows(11 - j))):
                    high, low = split(v)
                    lags[h, p, 0, at, lanes] = high
                    lags[h, p, 1, at, lanes] = low
            return 0

        lax.fori_loop(0, 8, window, 0)

    def product(h, quarter, p, first, last):
        at = pl.ds(pl.multiple_of(quarter * 256, 256), 256)
        lanes = pl.ds(first * 512, (last - first) * 512)
        total = None
        for i, j in ((0, 0), (0, 1), (1, 0)):
            term = lax.dot_general(lags[h, p, i, :, lanes], band[p, j, at, lanes], NT, preferred_element_type=F32)
            total = term if total is None else total + term
        return total

    def add_products(h, quarter, first, last, fresh=False, between=None):
        chunk = h * 4 + quarter
        for p, odds in ((0, (0, 1)), (1, (0,)), (2, (1,))):
            total = product(h, quarter, p, first, last)
            for m in range(8):
                for b in odds:
                    to_x, to_y = 2 * (m % 2) + b, m // 2
                    block = total[m * 32:(m + 1) * 32, :]
                    for way, (one, two) in enumerate(((to_x, to_y), (to_y, to_x))):
                        v = block[:, way * 128:(way + 1) * 128]
                        if p == 2:
                            v = part[chunk, way, one, two] - v
                        elif p == 1 or not fresh:
                            v = part[chunk, way, one, two] + v
                        part[chunk, way, one, two] = v
            if between is not None:
                between(p)

    ring, at_ring = (on_x, on_y), (xs, ys)

    def stage1(chunk, way, d):
        return remote(part.at[chunk, way, at_ring[way][d]], got1.at[chunk, way, d - 1],
                      send1.at[chunk, way, d - 1, 0], recv1.at[chunk, way, d - 1, 0], ring[way][d])

    def relay(chunk, way, kind, turn):
        d = 3 if turn else 1
        half = 1 - turn if kind == 1 else turn
        owner = at_ring[way][2 if kind == 0 else d]
        return remote(part.at[chunk, way, owner, pl.ds(2 * half, 2)], got1.at[chunk, way, kind, pl.ds(2 * half, 2)],
                      send1.at[chunk, way, kind, turn], recv1.at[chunk, way, kind, turn], ring[way][d])

    def stage2(chunk, way, d):
        return remote(part.at[chunk, way, at_ring[way][0], at_ring[1 - way][d]], got2.at[chunk, way, d - 1],
                      send2.at[chunk, way, d - 1], recv2.at[chunk, way, d - 1], ring[1 - way][d])

    both = [(way, turn) for way in range(2) for turn in range(2)]

    def begin(chunk):
        for kind in (0, 1):
            for way, turn in both:
                relay(chunk, way, kind, turn).start()

    def pass_sums(chunk):
        for way, turn in both:
            relay(chunk, way, 0, turn).wait_recv()
        for way, turn in both:
            owner = at_ring[way][3 if turn else 1]
            part[chunk, way, owner, 2 * turn:2 * turn + 2] += got1[chunk, way, 0, 2 * turn:2 * turn + 2]
        for way, turn in both:
            relay(chunk, way, 2, turn).start()

    def begin_direct(chunk):
        for d in (2, 1, 3):
            for way in range(2):
                stage1(chunk, way, d).start()

    def second(chunk):
        for d in (2, 1, 3):
            for way in range(2):
                stage2(chunk, way, d).start()

    def cross(chunk):
        for way, turn in both:
            relay(chunk, way, 1, turn).wait_recv()
            relay(chunk, way, 2, turn).wait_recv()
        for way in range(2):
            part[chunk, way, at_ring[way][0]] += got1[chunk, way, 1] + got1[chunk, way, 2]
        second(chunk)

    def cross_direct(chunk):
        for way in range(2):
            for d in (1, 3, 2):
                stage1(chunk, way, d).wait_recv()
        for way in range(2):
            part[chunk, way, at_ring[way][0]] += got1[chunk, way, 0] + (got1[chunk, way, 1] + got1[chunk, way, 2])
        second(chunk)

    def finish(h, quarter):
        chunk = h * 4 + quarter
        for way in range(2):
            for d in (1, 3, 2):
                stage2(chunk, way, d).wait_recv()
            v = ((part[chunk, way, at_ring[way][0], at_ring[1 - way][0]] + got2[chunk, way, 0])
                 + (got2[chunk, way, 1] + got2[chunk, way, 2]))
            out[:, h * 8:(h + 1) * 8, quarter * 256 + way * 128:quarter * 256 + way * 128 + 128] = v.reshape(4, 8, 128)

    def gather(h):
        for d in (1, 3, 2):
            to_z(h, d).start()

    def pass_on(h, places):
        for place in places:
            o = OFFSETS[place]
            to_z(h, 4 - o).wait_recv()
            to_pair(h, o).start()

    def arrive(h, places):
        for place in places:
            to_pair(h, OFFSETS[place]).wait_recv()
            split_lags(h, place)

    fetch(0, 0).wait()
    split_band(0, 0)
    fetch(2, 0).start()
    fetch(1, 1).wait()
    split_band(1, 1)
    fetch(3, 1).start()
    fetch(2, 0).wait()
    split_band(2, 0)
    pl.semaphore_wait(barrier, len(partners))
    gather(0)
    for h in range(2):
        to_pair(h, 0).start()
    fetch(3, 1).wait()
    split_band(3, 1)

    def own(h, first, count):
        def step(i, _):
            for n in range(count):
                add_products(h, first + i * count + n, 0, 1, fresh=True)
            return 0

        return step

    arrive(0, (0,))
    lax.fori_loop(0, 2, own(0, 0, 2), 0)
    gather(1)
    arrive(1, (0,))
    lax.fori_loop(0, 1, own(1, 0, 2), 0)
    pass_on(0, (1, 2))
    lax.fori_loop(0, 1, own(1, 2, 2), 0)
    arrive(0, (1, 2))
    add_products(0, 0, 1, 3)
    pass_on(0, (3,))
    add_products(0, 1, 1, 3)
    arrive(0, (3,))
    for quarter in range(2):
        add_products(0, quarter, 3, 4)
        begin(quarter)

    def rest(chunk, _):
        @pl.when(chunk == 3)
        def _():
            pass_on(1, (1, 2, 3))

        @pl.when(chunk == 4)
        def _():
            arrive(1, (1, 2, 3))

        add_products(chunk // 4, lax.rem(chunk, 4), 1, 4)

        @pl.when(chunk < 7)
        def _():
            begin(chunk)

        pass_sums(chunk - 2)

        @pl.when(chunk >= 4)
        def _():
            cross(chunk - 4)
        return 0

    lax.fori_loop(2, 8, rest, 0)
    begin_direct(7)
    cross(4)
    pass_sums(6)
    cross(5)
    cross_direct(7)
    cross(6)
    for h in range(2):
        for quarter in range(4):
            finish(h, quarter)

    for h in range(2):
        for d in (1, 2, 3):
            to_z(h, d).wait_send()
        for o in range(4):
            to_pair(h, o).wait_send()

    def sent(chunk, _):
        for way, turn in both:
            for kind in range(3):
                relay(chunk, way, kind, turn).wait_send()
        return 0

    lax.fori_loop(0, 7, sent, 0)
    for way in range(2):
        for d in (1, 2, 3):
            stage1(7, way, d).wait_send()

    def sent_second(chunk, _):
        for way in range(2):
            for d in (1, 2, 3):
                stage2(chunk, way, d).wait_send()
        return 0

    lax.fori_loop(0, 8, sent_second, 0)


def on_device(response, focusing):
    dma = pltpu.SemaphoreType.DMA
    return pl.pallas_call(
        kernel,
        out_shape=jax.ShapeDtypeStruct((4, 16, 1024), F32),
        in_specs=[pl.BlockSpec(memory_space=pl.ANY), pl.BlockSpec(memory_space=pltpu.VMEM)],
        out_specs=pl.BlockSpec(memory_space=pltpu.VMEM),
        scratch_shapes=[
            pltpu.VMEM((2, 8, 1024, 128), F32),
            pltpu.VMEM((3, 2, 1024, 2048), BF16),
            pltpu.VMEM((2, 4, 2, 288, 128), F32),
            pltpu.VMEM((568, 128), F32),
            pltpu.VMEM((2, 3, 2, 256, 2048), BF16),
            pltpu.VMEM((8, 2, 4, 4, 32, 128), F32),
            pltpu.VMEM((8, 2, 3, 4, 32, 128), F32),
            pltpu.VMEM((8, 2, 3, 32, 128), F32),
            dma((4,)), dma((2, 3)), dma((2, 4)), dma((2, 4, 2)),
            dma((8, 2, 3, 2)), dma((8, 2, 3, 2)), dma((8, 2, 3)), dma((8, 2, 3)),
        ],
        compiler_params=pltpu.CompilerParams(
            collective_id=0, has_side_effects=True, vmem_limit_bytes=63 * 2**20),
    )(response, jnp.swapaxes(focusing, 1, 2))


def solution(mesh):
    in_specs = (P(None, "rcv", "src"), P(None, None, ("src", "rcv")))
    return jax.shard_map(
        on_device, mesh=mesh, in_specs=in_specs, out_specs=P("src", None, "rcv"), check_vma=False
    )
```

time: 65.7 us -> 62.9 us (0.957)
  Pallas kernels: 63.8 us -> 61 us
    pallas_call x1, Pallas kernels: 63.8 us -> 61 us  [on_device(): pl.pallas_call(kernel, out_shape=jax.ShapeDtypeStruct((4, 16, 1024), F32)...]
where the time goes in v2:
time: 62.9 us; the launch traced here: 62.7 us
  Pallas kernels  61 us (97%)
  local copies, waits for them, and re-layouts  1.67 us (3%)
    pallas_call x1, Pallas kernels, on_device(): pl.pallas_call(kernel, out_shape=jax.ShapeDtypeStruct((4, 16, 1024), F32)...  61 us
    unnamed x1, local copies, waits for them, and re-layouts  1.67 us

profile of v2, /device:TPU:0, one launch (start us, length us, event | category | flops | bytes accessed | tf_op | source)
XLA Modules:
  0.0 62.7 jit_solution(7161756989918893715)
XLA Ops:
  0.0 61.0 %shard_map.28 = f32[4,16,1024]{2,1,0:T(8,128)} custom-call(f32[8,1024,512]{2,1,0:T(8,128)} %resp.1, f32[16,64,71]{2,1,0:T(8,128)} %bitcast.1), custom_call_target="tpu_custom_call" | custom-call | tf_op jit(solution)/shard_map/pallas_call | solution.py:309
  61.0 1.7 %copy.4 = f32[4,16,1024]{2,1,0:T(8,128)} copy(f32[4,16,1024]{2,1,0:T(8,128)} %shard_map.28) | data formatting | bytes 524288

commit v3 on v2

--- a/solution.py
+++ b/solution.py
@@ -206,20 +206,16 @@
             to_pair(h, OFFSETS[place]).wait_recv()
             split_lags(h, place)
 
+    pl.semaphore_wait(barrier, len(partners))
+    gather(0)
+    for h in range(2):
+        to_pair(h, 0).start()
     fetch(0, 0).wait()
     split_band(0, 0)
     fetch(2, 0).start()
     fetch(1, 1).wait()
     split_band(1, 1)
     fetch(3, 1).start()
-    fetch(2, 0).wait()
-    split_band(2, 0)
-    pl.semaphore_wait(barrier, len(partners))
-    gather(0)
-    for h in range(2):
-        to_pair(h, 0).start()
-    fetch(3, 1).wait()
-    split_band(3, 1)
 
     def own(h, first, count):
         def step(i, _):
@@ -231,18 +227,18 @@
 
     arrive(0, (0,))
     lax.fori_loop(0, 2, own(0, 0, 2), 0)
+    pass_on(0, (1, 2))
     gather(1)
+    fetch(2, 0).wait()
+    split_band(2, 0)
     arrive(1, (0,))
-    lax.fori_loop(0, 1, own(1, 0, 2), 0)
-    pass_on(0, (1, 2))
-    lax.fori_loop(0, 1, own(1, 2, 2), 0)
-    arrive(0, (1, 2))
-    add_products(0, 0, 1, 3)
+    lax.fori_loop(0, 2, own(1, 0, 2), 0)
     pass_on(0, (3,))
-    add_products(0, 1, 1, 3)
-    arrive(0, (3,))
+    fetch(3, 1).wait()
+    split_band(3, 1)
+    arrive(0, (1, 2, 3))
     for quarter in range(2):
-        add_products(0, quarter, 3, 4)
+        add_products(0, quarter, 1, 4)
         begin(quarter)
 
     def rest(chunk, _):

time: 62.9 us -> 61.4 us (0.976)
  Pallas kernels: 61 us -> 59.6 us
    pallas_call x1, Pallas kernels: 61 us -> 59.6 us  [on_device(): pl.pallas_call(kernel, out_shape=jax.ShapeDtypeStruct((4, 16, 1024), F32)...]
where the time goes in v3:
time: 61.4 us; the launch traced here: 61.3 us
  Pallas kernels  59.6 us (97%)
  local copies, waits for them, and re-layouts  1.67 us (3%)
    pallas_call x1, Pallas kernels, on_device(): pl.pallas_call(kernel, out_shape=jax.ShapeDtypeStruct((4, 16, 1024), F32)...  59.6 us
    unnamed x1, local copies, waits for them, and re-layouts  1.67 us

profile of v3, /device:TPU:0, one launch (start us, length us, event | category | flops | bytes accessed | tf_op | source)
XLA Modules:
  0.0 61.3 jit_solution(14596471593870963420)
XLA Ops:
  0.0 59.6 %shard_map.28 = f32[4,16,1024]{2,1,0:T(8,128)} custom-call(f32[8,1024,512]{2,1,0:T(8,128)} %resp.1, f32[16,64,71]{2,1,0:T(8,128)} %bitcast.1), custom_call_target="tpu_custom_call" | custom-call | tf_op jit(solution)/shard_map/pallas_call | solution.py:305
  59.6 1.7 %copy.4 = f32[4,16,1024]{2,1,0:T(8,128)} copy(f32[4,16,1024]{2,1,0:T(8,128)} %shard_map.28) | data formatting | bytes 524288

commit v4 on v3

--- a/solution.py
+++ b/solution.py
@@ -268,11 +268,13 @@
     cross(4)
     pass_sums(6)
     cross(5)
+    for quarter in range(3):
+        finish(0, quarter)
     cross_direct(7)
     cross(6)
-    for h in range(2):
-        for quarter in range(4):
-            finish(h, quarter)
+    finish(0, 3)
+    for quarter in range(4):
+        finish(1, quarter)
 
     for h in range(2):
         for d in (1, 2, 3):

time: 61.4 us -> 61.4 us (level)
  no operation moved by 1% of the time
where the time goes in v4:
time: 61.4 us; the launch traced here: 61.3 us
  Pallas kernels  59.6 us (97%)
  local copies, waits for them, and re-layouts  1.67 us (3%)
    pallas_call x1, Pallas kernels, on_device(): pl.pallas_call(kernel, out_shape=jax.ShapeDtypeStruct((4, 16, 1024), F32)...  59.6 us
    unnamed x1, local copies, waits for them, and re-layouts  1.67 us

profile of v4, /device:TPU:0, one launch (start us, length us, event | category | flops | bytes accessed | tf_op | source)
XLA Modules:
  0.0 61.3 jit_solution(10577963868887815119)
XLA Ops:
  0.0 59.6 %shard_map.28 = f32[4,16,1024]{2,1,0:T(8,128)} custom-call(f32[8,1024,512]{2,1,0:T(8,128)} %resp.1, f32[16,64,71]{2,1,0:T(8,128)} %bitcast.1), custom_call_target="tpu_custom_call" | custom-call | tf_op jit(solution)/shard_map/pallas_call | solution.py:307
  59.6 1.7 %copy.4 = f32[4,16,1024]{2,1,0:T(8,128)} copy(f32[4,16,1024]{2,1,0:T(8,128)} %shard_map.28) | data formatting | bytes 524288
